TPU v7x, 32 devices: a whole 2x2x4 slice. The times are simulated.
32 devices in a mesh: ctx: 16 (over z, x, core), tp: 2 (over y).
Axes of the slice: x: 2, y: 2, z: 4, core: 2. Of those that a mesh axis runs over, the one named last changes fastest.
Arguments:
- token_ids: int32 [2048], P('ctx'), may hold values from 0 to 511
- stream_table: bfloat16 [3, 512, 4096], P(None, None, 'tp'), may hold values from -6 to 6
- filters: float32 [256, 128], P('tp'), may hold values from -4 to 4
- proj_qk: bfloat16 [4096, 2, 4096], P(None, None, 'tp'), may hold values from -4 to 4
Outputs:
- attended: bfloat16 [2048, 4096], P('ctx', 'tp')
All inputs are finite; a program needn't handle non-finite values.
Results may differ from a plain program's by a relative error of at most 0.01.
Values may be sent and summed in bfloat16 or wider, within the bound.
A program may use at most 128 MiB of HBM per device.

v0:
```python
import jax
import jax.numpy as jnp
from jax import lax
from jax.sharding import PartitionSpec as P

HEAD = 128
GROUP = 16
FLEN = 128
SPAN = 8


def from_behind(value, axis, steps):
    count = lax.axis_size(axis)
    leading, last = (max(0, -steps), min(count, count - steps))
    return lax.ppermute(value, axis, [(source, source + steps) for source in range(leading, last)])


def attend(state_now, queries, key_value, key_offset, query_offset, lowest):
    row_max, row_sum, numerator = state_now
    tok_rows = queries.shape[0]
    head_count = row_max.shape[0]
    span_rows = key_value.shape[1]
    query_heads = queries.reshape(tok_rows, head_count, HEAD)
    key_heads = key_value[0].reshape(span_rows, head_count, HEAD)
    value_heads = key_value[1].reshape(span_rows, head_count, HEAD)
    scores = jnp.einsum(
        "thd,shd->hts", query_heads, key_heads, preferred_element_type=jnp.float32
    ) * HEAD ** (-0.5)
    key_pos = key_offset + jnp.arange(span_rows, dtype=jnp.int32)
    query_pos = query_offset + jnp.arange(tok_rows, dtype=jnp.int32)
    allowed = (key_pos[None, :] >= lowest) & (key_pos[None, :] <= query_pos[:, None])
    masked = jnp.where(allowed[None], scores, -1e30)
    new_max = jnp.maximum(row_max, jnp.max(masked, axis=2))
    rescale = jnp.exp(row_max - new_max)
    weights = jnp.where(allowed[None], jnp.exp(masked - new_max[:, :, None]), 0.0)
    row_sum = row_sum * rescale + jnp.sum(weights, axis=2)
    partial_out = jnp.einsum(
        "hts,shd->thd",
        weights.astype(jnp.bfloat16),
        value_heads,
        preferred_element_type=jnp.float32,
    )
    numerator = numerator * jnp.transpose(rescale)[:, :, None] + partial_out
    return (new_max, row_sum, numerator)


def toeplitz_taps(filters):
    groups_here = filters.shape[0]
    padded_taps = jnp.concatenate(
        [
            jnp.zeros((groups_here, 1), jnp.float32),
            filters[:, ::-1],
            jnp.zeros((groups_here, FLEN), jnp.float32),
        ],
        axis=1,
    )
    tiled = jnp.tile(padded_taps, (1, FLEN))[:, : FLEN * 2 * FLEN]
    return tiled.reshape(groups_here, FLEN, 2 * FLEN)


def shards(token_ids, stream_table, filters, proj_qk):
    tok_rows = token_ids.shape[0]
    chan_width = stream_table.shape[2]
    onehot = (
        token_ids[:, None] == jnp.arange(stream_table.shape[1], dtype=jnp.int32)[None, :]
    ).astype(jnp.bfloat16)
    streams = jnp.einsum("tv,svc->stc", onehot, stream_table, preferred_element_type=jnp.float32)
    mixed_in = (streams[1] * streams[2]).astype(jnp.bfloat16)
    rim_rows = from_behind(mixed_in[tok_rows - (FLEN - 1) :], "ctx", 1)
    extended = jnp.concatenate(
        [jnp.zeros((1, chan_width), jnp.bfloat16), rim_rows, mixed_in], axis=0
    )
    block_count = tok_rows // FLEN
    stacked = extended.reshape(block_count + 1, FLEN, chan_width).astype(jnp.float32)
    paired = jnp.concatenate([stacked[:-1], stacked[1:]], axis=1)
    groups_here = filters.shape[0]
    paired = paired.reshape(block_count, 2 * FLEN, groups_here, GROUP)
    toeplitz = toeplitz_taps(filters)
    conv = jnp.einsum("gos,nsgc->nogc", toeplitz, paired, precision=lax.Precision.HIGHEST).reshape(
        tok_rows, chan_width
    )
    gated = (streams[0] * conv).astype(jnp.bfloat16)
    weights_local = proj_qk.reshape(proj_qk.shape[0], 2 * chan_width)
    projected = jnp.dot(
        lax.all_gather(gated, "tp", axis=1, tiled=True),
        weights_local,
        preferred_element_type=jnp.float32,
    )
    queries = projected[:, :chan_width].astype(jnp.bfloat16)
    keys = projected[:, chan_width:].astype(jnp.bfloat16)
    head_count = chan_width // HEAD
    position = lax.axis_index("ctx")
    query_offset = position * tok_rows
    lowest = jnp.maximum(position - SPAN + 1, 0) * tok_rows
    key_value = jnp.stack([keys, gated])
    initial = (
        jnp.full((head_count, tok_rows), -1e30, jnp.float32),
        jnp.zeros((head_count, tok_rows), jnp.float32),
        jnp.zeros((tok_rows, head_count, HEAD), jnp.float32),
    )
    state_now = attend(initial, queries, key_value, query_offset, query_offset, lowest)
    moving = key_value
    for distance in range(1, SPAN):
        moving = from_behind(moving, "ctx", 1)
        state_now = attend(
            state_now, queries, moving, query_offset - distance * tok_rows, query_offset, lowest
        )
    row_max, row_sum, numerator = state_now
    result = numerator / jnp.transpose(row_sum)[:, :, None]
    return result.reshape(tok_rows, chan_width).astype(jnp.bfloat16)


def solution(mesh):
    placed = (P("ctx"), P(None, None, "tp"), P("tp", None), P(None, None, "tp"))
    return jax.shard_map(
        shards, mesh=mesh, in_specs=placed, out_specs=P("ctx", "tp"), check_vma=False
    )
```

profile of v0, /device:TPU:11, one launch (start us, length us, event | category | flops | bytes accessed | tf_op | source)
XLA Modules:
  0.0 285.6 jit_solution(15078711216360552776)
XLA Ops:
  6.5 3.8 %convolution_bitcast_fusion = f32[3,128,2048]{2,1,0:T(8,128)S(1)} fusion(bf16[3,512,2048]{2,1,0:T(8,128)(2,1)} %param.5, s32[128]{0:T(128)} %param.4), kind=kOutput, calls=%fused_computation.1 | convolution fusion | flops 805371904 | bytes 9437696 | tf_op jit(solution)/shard_map/tv,svc->stc/dot_general | solution.py:67
  11.4 3.7 %collective-permute-start = (bf16[127,2048]{1,0:T(8,128)(2,1)}, bf16[127,2048]{1,0:T(8,128)(2,1)}, u32[]{:S(2)}, u32[]{:S(2)}) collective-permute-start(bf16[127,2048]{1,0:T(8,128)(2,1)} %slice_bitcast_fusion.10), channel_id=1, source_target_pairs={{0,2},{2,4},{4,6},{6,8},{8,10},{10,12},{12,14},{14,16},{16,18},{18... | collective-permute-start | bytes 1560584 | tf_op jit(solution)/shard_map/ppermute | solution.py:15
  15.5 7.0 %tile.4 = f32[128,128,257]{0,2,1:T(8,128)} broadcast(f32[128,257]{0,1:T(8,128)S(1)} %copy.42), dimensions={0,2} | broadcast | bytes 16974336 | tf_op jit(solution)/shard_map/tile | solution.py:57
  22.6 17.5 %tile.10 = f32[128,32896]{0,1:T(8,128)} reshape(f32[128,128,257]{0,2,1:T(8,128)} %tile.4) | data formatting | bytes 33685504 | tf_op jit(solution)/shard_map/tile | solution.py:57
  40.1 11.3 %slice.112 = f32[128,32768]{0,1:T(8,128)} slice(f32[128,32896]{0,1:T(8,128)} %tile.10), slice={[0:128], [0:32768]} | slice | bytes 33554432 | tf_op jit(solution)/shard_map/slice | solution.py:57
  51.4 17.7 %copy.87 = f32[128,128,256]{2,1,0:T(8,128)} copy(f32[128,128,256]{0,2,1:T(8,128)} %bitcast.293) | data formatting | bytes 33554432 | tf_op jit(solution)/shard_map/reshape | solution.py:58
  72.2 2.9 %copy.41 = f32[1,256,2048]{1,2,0:T(8,128)} copy(f32[1,256,2048]{2,1,0:T(8,128)} %pad_maximum_fusion) | data formatting | bytes 4194304 | tf_op jit(solution)/shard_map/concatenate | solution.py:75
  75.1 18.5 %fusion.141 = f32[128,16,128]{2,1,0:T(8,128)} fusion(f32[256,128,16]{0,2,1:T(8,128)} %bitcast.298, f32[128,128,256]{2,1,0:T(8,128)} %copy.87), kind=kOutput, calls=%fused_computation.225 | convolution fusion | flops 805306368 | bytes 19922944 | tf_op jit(solution)/shard_map/gos,nsgc->nogc/dot_general | solution.py:79
  93.6 2.6 copy.44
  98.3 23.3 %copy.98 = bf16[512,8,2,2048]{3,1,2,0:T(8,128)(2,1)} copy(bf16[512,8,2,2048]{3,2,1,0:T(2,128)(2,1)} %bitcast.294) | data formatting | bytes 67108864
  121.6 2.6 copy.49
  126.7 15.4 %convolution_convert_fusion = bf16[128,4096]{1,0:T(8,128)(2,1)S(1)} fusion(bf16[128,4096]{1,0:T(8,128)(2,1)} %all-gather.2.cloned.1.call-done, bf16[4096,4096]{1,0:T(8,128)(2,1)} %bitcast.292), kind=kOutput, calls=%fused_computation | convolution fusion | flops 4295491584 | bytes 35651584 | tf_op jit(solution)/shard_map/dot_general | solution.py:84
  145.4 11.7 %collective-permute-done.1 = bf16[2,128,2048]{2,1,0:T(8,128)(2,1)S(1)} collective-permute-done((bf16[2,128,2048]{2,1,0:T(8,128)(2,1)S(1)}, bf16[2,128,2048]{2,1,0:T(8,128)(2,1)S(1)}, u32[]{:S(2)}, u32[]{:S(2)}) %collective-permute-start.1) | collective-permute-done | bytes 1048608 | tf_op jit(solution)/shard_map/ppermute | solution.py:15
  157.1 5.3 %collective-permute-start.2 = (bf16[2,128,2048]{2,1,0:T(8,128)(2,1)S(1)}, bf16[2,128,2048]{2,1,0:T(8,128)(2,1)S(1)}, u32[]{:S(2)}, u32[]{:S(2)}) collective-permute-start(bf16[2,128,2048]{2,1,0:T(8,128)(2,1)S(1)} %collective-permute-done.1), channel_id=1, source_target_pairs={{0,2},{2,4},{4,6},{6,8},{8,10},{10,12},{12,14},{14,16},{16,18},{18... | collective-permute-start | bytes 3145736 | tf_op jit(solution)/shard_map/ppermute | solution.py:15
  162.4 11.7 %collective-permute-done.2 = bf16[2,128,2048]{2,1,0:T(8,128)(2,1)S(1)} collective-permute-done((bf16[2,128,2048]{2,1,0:T(8,128)(2,1)S(1)}, bf16[2,128,2048]{2,1,0:T(8,128)(2,1)S(1)}, u32[]{:S(2)}, u32[]{:S(2)}) %collective-permute-start.2) | collective-permute-done | bytes 1048608 | tf_op jit(solution)/shard_map/ppermute | solution.py:15
  174.1 5.3 %collective-permute-start.3 = (bf16[2,128,2048]{2,1,0:T(8,128)(2,1)S(1)}, bf16[2,128,2048]{2,1,0:T(8,128)(2,1)S(1)}, u32[]{:S(2)}, u32[]{:S(2)}) collective-permute-start(bf16[2,128,2048]{2,1,0:T(8,128)(2,1)S(1)} %collective-permute-done.2), channel_id=1, source_target_pairs={{0,2},{2,4},{4,6},{6,8},{8,10},{10,12},{12,14},{14,16},{16,18},{18... | collective-permute-start | bytes 3145736 | tf_op jit(solution)/shard_map/ppermute | solution.py:15
  179.6 11.6 %collective-permute-done.3 = bf16[2,128,2048]{2,1,0:T(8,128)(2,1)S(1)} collective-permute-done((bf16[2,128,2048]{2,1,0:T(8,128)(2,1)S(1)}, bf16[2,128,2048]{2,1,0:T(8,128)(2,1)S(1)}, u32[]{:S(2)}, u32[]{:S(2)}) %collective-permute-start.3) | collective-permute-done | bytes 1048608 | tf_op jit(solution)/shard_map/ppermute | solution.py:15
  191.1 5.3 %collective-permute-start.4 = (bf16[2,128,2048]{2,1,0:T(8,128)(2,1)S(1)}, bf16[2,128,2048]{2,1,0:T(8,128)(2,1)}, u32[]{:S(2)}, u32[]{:S(2)}) collective-permute-start(bf16[2,128,2048]{2,1,0:T(8,128)(2,1)S(1)} %collective-permute-done.3), channel_id=1, source_target_pairs={{0,2},{2,4},{4,6},{6,8},{8,10},{10,12},{12,14},{14,16},{16,18},{18... | collective-permute-start | bytes 3145736 | tf_op jit(solution)/shard_map/ppermute | solution.py:15
  198.1 2.7 fusion.140
  204.8 3.3 %collective-permute-done.4 = bf16[2,128,2048]{2,1,0:T(8,128)(2,1)} collective-permute-done((bf16[2,128,2048]{2,1,0:T(8,128)(2,1)S(1)}, bf16[2,128,2048]{2,1,0:T(8,128)(2,1)}, u32[]{:S(2)}, u32[]{:S(2)}) %collective-permute-start.4) | collective-permute-done | bytes 1048608 | tf_op jit(solution)/shard_map/ppermute | solution.py:15
  208.1 5.4 %collective-permute-start.5 = (bf16[2,128,2048]{2,1,0:T(8,128)(2,1)}, bf16[2,128,2048]{2,1,0:T(8,128)(2,1)}, u32[]{:S(2)}, u32[]{:S(2)}) collective-permute-start(bf16[2,128,2048]{2,1,0:T(8,128)(2,1)} %collective-permute-done.4), channel_id=1, source_target_pairs={{0,2},{2,4},{4,6},{6,8},{8,10},{10,12},{12,14},{14,16},{16,18},{18... | collective-permute-start | bytes 3145736 | tf_op jit(solution)/shard_map/ppermute | solution.py:15
  217.4 8.2 %collective-permute-done.5 = bf16[2,128,2048]{2,1,0:T(8,128)(2,1)} collective-permute-done((bf16[2,128,2048]{2,1,0:T(8,128)(2,1)}, bf16[2,128,2048]{2,1,0:T(8,128)(2,1)}, u32[]{:S(2)}, u32[]{:S(2)}) %collective-permute-start.5) | collective-permute-done | bytes 1048608 | tf_op jit(solution)/shard_map/ppermute | solution.py:15
  225.6 5.3 %collective-permute-start.6 = (bf16[2,128,2048]{2,1,0:T(8,128)(2,1)}, bf16[2,128,2048]{2,1,0:T(8,128)(2,1)}, u32[]{:S(2)}, u32[]{:S(2)}) collective-permute-start(bf16[2,128,2048]{2,1,0:T(8,128)(2,1)} %collective-permute-done.5), channel_id=1, source_target_pairs={{0,2},{2,4},{4,6},{6,8},{8,10},{10,12},{12,14},{14,16},{16,18},{18... | collective-permute-start | bytes 3145736 | tf_op jit(solution)/shard_map/ppermute | solution.py:15
  242.9 5.5 %collective-permute-start.7 = (bf16[2,128,2048]{2,1,0:T(8,128)(2,1)}, bf16[2,128,2048]{2,1,0:T(8,128)(2,1)}, u32[]{:S(2)}, u32[]{:S(2)}) collective-permute-start(bf16[2,128,2048]{2,1,0:T(8,128)(2,1)} %collective-permute-done.6), channel_id=1, source_target_pairs={{0,2},{2,4},{4,6},{6,8},{8,10},{10,12},{12,14},{14,16},{16,18},{18... | collective-permute-start | bytes 3145736 | tf_op jit(solution)/shard_map/ppermute | solution.py:15
  (122 shorter events, 64.2 us)
Async XLA Ops:
  6.5 120.2 %all-gather.2.cloned.1.call-start = ((), (), s32[]{:S(2)}) async-start(), calls=%async_computation | async-start | bytes 1572864 | tf_op jit(solution)/shard_map/all_gather | solution.py:85
  10.4 4.9 %copy-start.19 = (f32[128,128]{1,0:T(8,128)S(1)}, f32[128,128]{1,0:T(8,128)}, u32[]{:S(2)}) copy-start(f32[128,128]{1,0:T(8,128)} %param.6) | copy-start | bytes 196612
  11.4 57.8 %collective-permute-start = (bf16[127,2048]{1,0:T(8,128)(2,1)}, bf16[127,2048]{1,0:T(8,128)(2,1)}, u32[]{:S(2)}, u32[]{:S(2)}) collective-permute-start(bf16[127,2048]{1,0:T(8,128)(2,1)} %slice_bitcast_fusion.10), channel_id=1, source_target_pairs={{0,2},{2,4},{4,6},{6,8},{8,10},{10,12},{12,14},{14,16},{16,18},{18... | collective-permute-start | bytes 1560584 | tf_op jit(solution)/shard_map/ppermute | solution.py:15
  126.7 16.6 %copy-start.13 = (bf16[1,128,2048]{2,1,0:T(8,128)(2,1)S(1)}, bf16[1,128,2048]{2,1,0:T(8,128)(2,1)}, u32[]{:S(2)}) copy-start(bf16[1,128,2048]{2,1,0:T(8,128)(2,1)} %get-tuple-element.21) | copy-start | bytes 1572868
  142.2 54.6 %copy-start.1 = (f32[1,128,2048]{2,1,0:T(8,128)S(1)}, f32[1,128,2048]{2,1,0:T(8,128)}, u32[]{:S(2)}) copy-start(f32[1,128,2048]{2,1,0:T(8,128)} %get-tuple-element.22) | copy-start | bytes 3145732
  143.5 13.7 %collective-permute-start.1 = (bf16[2,128,2048]{2,1,0:T(8,128)(2,1)S(1)}, bf16[2,128,2048]{2,1,0:T(8,128)(2,1)S(1)}, u32[]{:S(2)}, u32[]{:S(2)}) collective-permute-start(bf16[2,128,2048]{2,1,0:T(8,128)(2,1)S(1)} %pad_maximum_fusion.1), channel_id=1, source_target_pairs={{0,2},{2,4},{4,6},{6,8},{8,10},{10,12},{12,14},{14,16},{16,18},{18... | collective-permute-start | bytes 3145736 | tf_op jit(solution)/shard_map/ppermute | solution.py:15
  157.1 17.0 %copy-start.16 = (bf16[2,128,2048]{2,1,0:T(8,128)(2,1)}, bf16[2,128,2048]{2,1,0:T(8,128)(2,1)S(1)}, u32[]{:S(2)}) copy-start(bf16[2,128,2048]{2,1,0:T(8,128)(2,1)S(1)} %collective-permute-done.1) | copy-start | bytes 3145732
  157.1 17.0 %collective-permute-start.2 = (bf16[2,128,2048]{2,1,0:T(8,128)(2,1)S(1)}, bf16[2,128,2048]{2,1,0:T(8,128)(2,1)S(1)}, u32[]{:S(2)}, u32[]{:S(2)}) collective-permute-start(bf16[2,128,2048]{2,1,0:T(8,128)(2,1)S(1)} %collective-permute-done.1), channel_id=1, source_target_pairs={{0,2},{2,4},{4,6},{6,8},{8,10},{10,12},{12,14},{14,16},{16,18},{18... | collective-permute-start | bytes 3145736 | tf_op jit(solution)/shard_map/ppermute | solution.py:15
  174.1 27.9 %copy-start.14 = (bf16[2,128,2048]{2,1,0:T(8,128)(2,1)}, bf16[2,128,2048]{2,1,0:T(8,128)(2,1)S(1)}, u32[]{:S(2)}) copy-start(bf16[2,128,2048]{2,1,0:T(8,128)(2,1)S(1)} %collective-permute-done.2) | copy-start | bytes 3145732
  174.1 17.0 %collective-permute-start.3 = (bf16[2,128,2048]{2,1,0:T(8,128)(2,1)S(1)}, bf16[2,128,2048]{2,1,0:T(8,128)(2,1)S(1)}, u32[]{:S(2)}, u32[]{:S(2)}) collective-permute-start(bf16[2,128,2048]{2,1,0:T(8,128)(2,1)S(1)} %collective-permute-done.2), channel_id=1, source_target_pairs={{0,2},{2,4},{4,6},{6,8},{8,10},{10,12},{12,14},{14,16},{16,18},{18... | collective-permute-start | bytes 3145736 | tf_op jit(solution)/shard_map/ppermute | solution.py:15
  191.1 17.0 %collective-permute-start.4 = (bf16[2,128,2048]{2,1,0:T(8,128)(2,1)S(1)}, bf16[2,128,2048]{2,1,0:T(8,128)(2,1)}, u32[]{:S(2)}, u32[]{:S(2)}) collective-permute-start(bf16[2,128,2048]{2,1,0:T(8,128)(2,1)S(1)} %collective-permute-done.3), channel_id=1, source_target_pairs={{0,2},{2,4},{4,6},{6,8},{8,10},{10,12},{12,14},{14,16},{16,18},{18... | collective-permute-start | bytes 3145736 | tf_op jit(solution)/shard_map/ppermute | solution.py:15
  203.1 10.4 %copy-start.15 = (bf16[2,128,2048]{2,1,0:T(8,128)(2,1)S(1)}, bf16[2,128,2048]{2,1,0:T(8,128)(2,1)}, u32[]{:S(2)}) copy-start(bf16[2,128,2048]{2,1,0:T(8,128)(2,1)} %copy-done.14) | copy-start | bytes 3145732
  208.1 17.4 %collective-permute-start.5 = (bf16[2,128,2048]{2,1,0:T(8,128)(2,1)}, bf16[2,128,2048]{2,1,0:T(8,128)(2,1)}, u32[]{:S(2)}, u32[]{:S(2)}) collective-permute-start(bf16[2,128,2048]{2,1,0:T(8,128)(2,1)} %collective-permute-done.4), channel_id=1, source_target_pairs={{0,2},{2,4},{4,6},{6,8},{8,10},{10,12},{12,14},{14,16},{16,18},{18... | collective-permute-start | bytes 3145736 | tf_op jit(solution)/shard_map/ppermute | solution.py:15
  214.7 16.2 %copy-start.17 = (bf16[16,16,8,128]{3,2,1,0:T(8,128)(2,1)S(1)}, bf16[16,16,8,128]{3,2,1,0:T(8,128)(2,1)}, u32[]{:S(2)}) copy-start(bf16[16,16,8,128]{3,2,1,0:T(8,128)(2,1)} %get-tuple-element.41) | copy-start | bytes 1572868
  225.6 17.3 %collective-permute-start.6 = (bf16[2,128,2048]{2,1,0:T(8,128)(2,1)}, bf16[2,128,2048]{2,1,0:T(8,128)(2,1)}, u32[]{:S(2)}, u32[]{:S(2)}) collective-permute-start(bf16[2,128,2048]{2,1,0:T(8,128)(2,1)} %collective-permute-done.5), channel_id=1, source_target_pairs={{0,2},{2,4},{4,6},{6,8},{8,10},{10,12},{12,14},{14,16},{16,18},{18... | collective-permute-start | bytes 3145736 | tf_op jit(solution)/shard_map/ppermute | solution.py:15
  242.9 21.4 %collective-permute-start.7 = (bf16[2,128,2048]{2,1,0:T(8,128)(2,1)}, bf16[2,128,2048]{2,1,0:T(8,128)(2,1)}, u32[]{:S(2)}, u32[]{:S(2)}) collective-permute-start(bf16[2,128,2048]{2,1,0:T(8,128)(2,1)} %collective-permute-done.6), channel_id=1, source_target_pairs={{0,2},{2,4},{4,6},{6,8},{8,10},{10,12},{12,14},{14,16},{16,18},{18... | collective-permute-start | bytes 3145736 | tf_op jit(solution)/shard_map/ppermute | solution.py:15
  268.7 3.2 %copy-start.4 = (f32[16,128,128]{1,2,0:T(8,128)S(1)}, f32[16,128,128]{1,2,0:T(8,128)}, u32[]{:S(2)}) copy-start(f32[16,128,128]{1,2,0:T(8,128)} %get-tuple-element.56) | copy-start | bytes 3145732
  268.7 3.4 %copy-start.3 = (f32[16,128,128]{1,2,0:T(8,128)S(1)}, f32[16,128,128]{1,2,0:T(8,128)}, u32[]{:S(2)}) copy-start(f32[16,128,128]{1,2,0:T(8,128)} %get-tuple-element.58) | copy-start | bytes 3145732
  270.0 2.3 copy-start.2
  271.9 1.3 copy-start.6
  272.1 1.4 copy-start
  272.1 1.7 copy-start.5
  272.9 1.2 copy-start.7
  276.3 1.1 copy-start.18
  (5 other events, 5.4 us)
Sparse Core Ops, SparseCore 0:
  98.4 20.9 all-gather.1
where the time goes:
time: 288 us; the launch traced here: 286 us
  local copies, waits for them, and re-layouts  120 us (42%)
  matrix products  55.8 us (19%)
  waiting for transfers between devices  48 us (17%)
  starting transfers between devices  37.6 us (13%)
  between operations  13.9 us (5%)
  other arithmetic  10 us (3%)
    ppermute x8, waiting for transfers between devices, from_behind(): lax.ppermute(value, axis, [(source, source + steps) for source in range(l...  48 us
    ppermute x8, starting transfers between devices, from_behind(): lax.ppermute(value, axis, [(source, source + steps) for source in range(l...  37.6 us
    unnamed x48, local copies, waits for them, and re-layouts  30.1 us
    another operation x2, local copies, waits for them, and re-layouts, toeplitz_taps(): tiled = jnp.tile(padded_taps, (1, FLEN))[:, :FLEN * 2 * FLEN]  24.6 us
    dot_general x1, matrix products, shards(): jnp.einsum('gos,nsgc->nogc', toeplitz, paired, precision=lax.Precision.HI...  18.5 us
    reshape x1, local copies, waits for them, and re-layouts, toeplitz_taps(): return tiled.reshape(groups_here, FLEN, 2 * FLEN)  17.7 us
    dot_general x8, matrix products, attend(): jnp.einsum('thd,shd->hts', query_heads, key_heads, preferred_element_type...  15.5 us
    dot_general x1, matrix products, shards(): jnp.dot(lax.all_gather(gated, 'tp', axis=1, tiled=True), weights_local, p...  15.4 us
  transfers between devices with their start and end apart: 9, of which 6 were waited for; matrix products, arithmetic and copies ran while one was open for 42% of the time, Pallas kernels for 0%

commit v1 on v0

v1 whole, which is shorter than its diff:
```python
import functools
import jax
import jax.numpy as jnp
from jax import lax
from jax.experimental import pallas as pl
from jax.experimental.pallas import tpu as pltpu
from jax.sharding import PartitionSpec as P

HEAD = 128
GROUP = 16
FLEN = 128
SPAN = 8
LANE = 128
PLANE = 4
BACK = SPAN - 1
SLOTS = BACK + PLANE
MESH = pl.DeviceIdType.MESH
F32, BF16 = jnp.float32, jnp.bfloat16


def lanes(index, width=LANE):
    return pl.ds(pl.multiple_of(index * width, LANE), width)


def rows(index, count=1):
    return pl.ds(pl.multiple_of(index * FLEN, FLEN), count * FLEN)


def dot(a, b):
    return jnp.dot(a, b, preferred_element_type=F32)


def wait_ahead(barrier, ahead, always, each):
    for planes in range(3):
        @pl.when(ahead == planes if planes < 2 else ahead >= planes)
        def _():
            pl.semaphore_wait(barrier, always + planes * each)


def ids_kernel(count, ids_ref, out_ref, buf, send, recv):
    me = lax.axis_index("ctx")
    plane, place = me // PLANE, me % PLANE
    planes = count // PLANE
    buf[...] = jnp.full(buf.shape, -1, jnp.int32)
    buf[2 * PLANE + place] = ids_ref[...]
    barrier = pltpu.get_barrier_semaphore()

    def partners(sign, act):
        for dist in range(3):
            for other in range(PLANE):
                there = plane + sign * dist
                ok = (there >= 0) & (there < planes)
                if dist == 0:
                    ok = ok & (other != place)
                pl.when(ok)(functools.partial(act, dist, other, there * PLANE + other))

    def greet(dist, other, device):
        pl.semaphore_signal(barrier, inc=1, device_id={"ctx": device}, device_id_type=MESH)

    def copy_to(dist, other, device):
        return pltpu.make_async_remote_copy(
            src_ref=ids_ref,
            dst_ref=buf.at[2 * PLANE + place - dist * PLANE],
            send_sem=send.at[dist * PLANE + other],
            recv_sem=recv.at[2 * PLANE + place - dist * PLANE],
            device_id={"ctx": device},
            device_id_type=MESH,
        )

    def arrived(dist, other, device):
        slot = 2 * PLANE + other - dist * PLANE
        pltpu.make_async_remote_copy(
            src_ref=ids_ref, dst_ref=buf.at[slot], send_sem=send.at[0], recv_sem=recv.at[slot],
            device_id={"ctx": device}, device_id_type=MESH,
        ).wait_recv()

    partners(-1, greet)
    wait_ahead(barrier, planes - 1 - plane, PLANE - 1, PLANE)
    partners(1, lambda *a: copy_to(*a).start())
    partners(-1, arrived)
    partners(1, lambda *a: copy_to(*a).wait_send())
    out_ref[...] = buf[...]


def share_ids(token_ids, count):
    return pl.pallas_call(
        functools.partial(ids_kernel, count),
        out_shape=jax.ShapeDtypeStruct((3 * PLANE, 1, FLEN), jnp.int32),
        in_specs=[pl.BlockSpec(memory_space=pltpu.VMEM)],
        out_specs=pl.BlockSpec(memory_space=pltpu.VMEM),
        scratch_shapes=[
            pltpu.VMEM((3 * PLANE, 1, FLEN), jnp.int32),
            pltpu.SemaphoreType.DMA((3 * PLANE,)),
            pltpu.SemaphoreType.DMA((3 * PLANE,)),
        ],
        compiler_params=pltpu.CompilerParams(collective_id=0, has_side_effects=True),
        name="share_ids",
    )(token_ids.reshape(1, FLEN))


def conv_kernel(ids_ref, table_ref, taps_ref, gated_ref, value_ref, onehot, toep, mixed, post):
    width = gated_ref.shape[1]
    part = value_ref.shape[1]
    vocab = table_ref.shape[1]
    place = lax.axis_index("ctx") % PLANE

    def mark(block, _):
        ids = jnp.transpose(jnp.broadcast_to(ids_ref[block].astype(F32), (FLEN, FLEN)))
        word = lax.broadcasted_iota(jnp.int32, (FLEN, LANE), 1).astype(F32)
        for at in range(vocab // LANE):
            onehot[rows(block), at * LANE:(at + 1) * LANE] = (ids == word + float(at * LANE)).astype(F32).astype(BF16)
        return 0

    lax.fori_loop(0, 3 * PLANE, mark, 0)
    tap = lax.broadcasted_iota(jnp.int32, (FLEN, 2 * FLEN), 0)
    spot = lax.broadcasted_iota(jnp.int32, (FLEN, 2 * FLEN), 1)
    flip = (spot + tap == FLEN).astype(F32).astype(BF16)
    per = LANE // GROUP

    def build(column):
        line = dot(taps_ref[pl.ds(pl.multiple_of(column * per, per), per), :].astype(BF16), flip)
        for g in range(per):
            spread = jnp.broadcast_to(line[g:g + 1], (FLEN, 2 * FLEN))
            toep[g * FLEN:(g + 1) * FLEN] = pltpu.roll(spread, 0, 1, stride=1, stride_axis=0).astype(BF16)

    group_of = lax.broadcasted_iota(jnp.int32, (FLEN, LANE), 1) // GROUP

    def convolve(window):
        every = dot(toep[...], window)
        total = every[:FLEN]
        for g in range(1, per):
            total = jnp.where(group_of == g, every[g * FLEN:(g + 1) * FLEN], total)
        return total

    def own(column, _):
        cols = lanes(column)
        pair = jnp.concatenate([table_ref[1, :, cols], table_ref[2, :, cols]], axis=1)
        both = dot(onehot[rows(BACK + place, 2), :], pair)
        window = (both[:, :LANE] * both[:, LANE:]).astype(BF16)
        gate = dot(onehot[rows(BACK + 1 + place), :], table_ref[0, :, cols])
        build(column)
        gated_ref[:, cols] = (gate * convolve(window)).astype(BF16)
        return 0

    lax.fori_loop(0, width // LANE, own, 0)

    def shared(step, _):
        column = place * (part // LANE) + step
        cols = lanes(column)
        pair = jnp.concatenate([table_ref[1, :, cols], table_ref[2, :, cols]], axis=1)
        build(column)

        def fill(block, _):
            marks = onehot[rows(block), :]
            both = dot(marks, pair)
            mixed[rows(block), :] = (both[:, :LANE] * both[:, LANE:]).astype(BF16)
            post[rows(block), :] = dot(marks, table_ref[0, :, cols])
            return 0

        lax.fori_loop(0, 3 * PLANE, fill, 0)

        def window_of(block, _):
            conv = convolve(mixed[rows(block, 2), :])
            value_ref[rows(block), lanes(step)] = (post[rows(block + 1), :] * conv).astype(BF16)
            return 0

        lax.fori_loop(0, SLOTS, window_of, 0)
        return 0

    lax.fori_loop(0, part // LANE, shared, 0)


def gated_and_values(ids, table, filters):
    width = table.shape[2]
    vmem = pl.BlockSpec(memory_space=pltpu.VMEM)
    return pl.pallas_call(
        conv_kernel,
        out_shape=(
            jax.ShapeDtypeStruct((FLEN, width), BF16),
            jax.ShapeDtypeStruct((SLOTS * FLEN, width // PLANE), BF16),
        ),
        in_specs=[vmem] * 3,
        out_specs=(vmem, vmem),
        scratch_shapes=[
            pltpu.VMEM((3 * PLANE * FLEN, table.shape[1]), BF16),
            pltpu.VMEM((LANE // GROUP * FLEN, 2 * FLEN), BF16),
            pltpu.VMEM((3 * PLANE * FLEN, LANE), BF16),
            pltpu.VMEM((3 * PLANE * FLEN, LANE), F32),
        ],
        compiler_params=pltpu.CompilerParams(vmem_limit_bytes=40 << 20),
        name="gated_and_values",
    )(ids, table, filters)


def attend_kernel(
    count, shares, gated_ref, value_ref, weight_ref, out_ref,
    gall, wide, held, acc, qsend, ksend, qbuf, kbuf, osend, obuf,
    gs, gr, ws, qs, qr, ks, kr, zs, os_, or_,
):
    width = gated_ref.shape[1]
    heads = width // HEAD
    part = width // PLANE
    heads_part = heads // PLANE
    me, mine = lax.axis_index("ctx"), lax.axis_index("tp")
    plane, place = me // PLANE, me % PLANE
    planes = count // PLANE

    def weights_copy(share, head):
        return pltpu.make_async_copy(
            weight_ref.at[pl.ds(share * width, width), head],
            held.at[head, pl.ds(share * width, width)],
            ws.at[share, head],
        )

    for step in range(shares):
        for head in range(heads):
            weights_copy((mine + step) % shares, head).start()

    kbuf[:BACK * FLEN] = jnp.zeros((BACK * FLEN, part), BF16)
    barrier = pltpu.get_barrier_semaphore()

    def greet(**device):
        pl.semaphore_signal(barrier, inc=1, device_id=device, device_id_type=MESH)

    for step in range(1, shares):
        greet(tp=(mine + step) % shares)
    for step in range(1, PLANE):
        greet(ctx=plane * PLANE + (place + step) % PLANE)
    for dist in (1, 2):
        @pl.when(plane >= dist)
        def _():
            greet(ctx=me - dist * PLANE)
    wait_ahead(barrier, planes - 1 - plane, shares - 1 + PLANE - 1, 1)

    def remote(src, dst, send, recv, **device):
        return pltpu.make_async_remote_copy(
            src_ref=src, dst_ref=dst, send_sem=send, recv_sem=recv, device_id=device, device_id_type=MESH
        )

    def gated_copy(step, slot):
        return remote(gated_ref, gall.at[slot], gs.at[step], gr.at[slot], tp=(mine + step) % shares)

    for step in range(1, shares):
        gated_copy(step, mine).start()
    gall[mine] = gated_ref[...]

    src = lax.broadcasted_iota(jnp.int32, (LANE, 4 * LANE), 0)
    dst = lax.broadcasted_iota(jnp.int32, (LANE, 4 * LANE), 1)
    spread = (dst == jnp.where(dst < 2 * LANE, 2 * src, 2 * src + 1 + 2 * LANE)).astype(F32).astype(BF16)
    paired = held.reshape(heads, 2 * shares * width, HEAD)
    depth = min(2 * width, 1024)

    def q_copy(group, slot):
        return remote(qsend.at[group], qbuf.at[slot], qs.at[group], qr.at[slot], ctx=plane * PLANE + group)

    def k_copy(group, slot):
        return remote(ksend.at[group], kbuf.at[rows(BACK + slot)], ks.at[group], kr.at[BACK + slot], ctx=plane * PLANE + group)

    def z_copy(dist, slot):
        to = BACK + slot - dist * PLANE
        return remote(kbuf.at[rows(BACK + slot)], kbuf.at[rows(to)], zs.at[dist - 1, slot], kr.at[to], ctx=me + dist * PLANE)

    def pass_on(slot, act):
        @pl.when(plane + 1 < planes)
        def _():
            act(z_copy(1, slot))

        @pl.when((plane + 2 < planes) & (slot >= 1))
        def _():
            act(z_copy(2, slot))

    def project(step, share, head):
        base = share * 2 * width

        def chunk(at, total):
            take = pl.ds(pl.multiple_of(base + at * depth, LANE), depth)
            block = jnp.concatenate([paired[head, take, :], paired[head + 1, take, :]], axis=1)
            return total + dot(wide[:, lanes(at, depth)], block)

        first = jnp.zeros((2 * FLEN, 2 * HEAD), F32) if step == 0 else acc[head // 2]
        return lax.fori_loop(0, 2 * width // depth, chunk, first)

    for step in range(shares):
        share = (mine + step) % shares
        if step > 0:
            gated_copy(step, share).wait_recv()

        def widen(column, _):
            both = dot(gall[share, :, lanes(column)], spread).astype(BF16)
            wide[:FLEN, lanes(column, 2 * LANE)] = both[:, :2 * LANE]
            wide[FLEN:, lanes(column, 2 * LANE)] = both[:, 2 * LANE:]
            return 0

        lax.fori_loop(0, width // LANE, widen, 0)
        for head in range(0, heads, 2):
            weights_copy(share, head).wait()
            weights_copy(share, head + 1).wait()
            total = project(step, share, head)
            if step < shares - 1:
                acc[head // 2] = total
                continue
            for one in range(2):
                group, at = (head + one) // heads_part, (head + one) % heads_part
                cut = total[:, one * HEAD:(one + 1) * HEAD].astype(BF16)
                qsend[group, :, at * HEAD:(at + 1) * HEAD] = cut[:FLEN]
                ksend[group, :, at * HEAD:(at + 1) * HEAD] = cut[FLEN:]
                if at == heads_part - 1:
                    @pl.when(group != place)
                    def _():
                        k_copy(group, place).start()
                        q_copy(group, place).start()

                    @pl.when(group == place)
                    def _():
                        kbuf[rows(BACK + place), :] = ksend[group]
                        qbuf[place] = qsend[group]
                        pass_on(place, lambda c: c.start())

    for step in range(1, PLANE):
        slot = (place + step) % PLANE
        k_copy(slot, slot).wait_recv()
        pass_on(slot, lambda c: c.start())
    for step in range(1, PLANE):
        slot = (place + step) % PLANE
        q_copy(slot, slot).wait_recv()
    for dist in (1, 2):
        @pl.when(plane >= dist)
        def _():
            for slot in range(dist - 1, PLANE):
                z_copy(dist, slot).wait_recv()

    def o_copy(group, slot):
        return remote(osend.at[group], obuf.at[slot], os_.at[group], or_.at[slot], ctx=plane * PLANE + group)

    key_at = lax.broadcasted_iota(jnp.int32, (FLEN, SPAN * FLEN), 1)
    query_at = lax.broadcasted_iota(jnp.int32, (FLEN, SPAN * FLEN), 0)
    for block in range(PLANE):
        least = (BACK - block - plane * PLANE) * FLEN
        allowed = (key_at <= query_at + BACK * FLEN) & (key_at >= least)

        def one_head(head, _):
            keys = kbuf[block * FLEN:(block + SPAN) * FLEN, lanes(head)]
            values = value_ref[block * FLEN:(block + SPAN) * FLEN, lanes(head)]
            scores = lax.dot_general(
                qbuf[block, :, lanes(head)], keys, (((1,), (1,)), ((), ())), preferred_element_type=F32
            ) * HEAD ** (-0.5)
            scores = jnp.where(allowed, scores, -1e30)
            weights = jnp.exp(scores - jnp.max(scores, axis=1, keepdims=True))
            row_sum = jnp.sum(weights, axis=1, keepdims=True)
            osend[block, :, lanes(head)] = (dot(weights.astype(BF16), values) / row_sum).astype(BF16)
            return 0

        lax.fori_loop(0, heads_part, one_head, 0)

        @pl.when(block != place)
        def _():
            o_copy(block, place).start()

        @pl.when(block == place)
        def _():
            obuf[place] = osend[block]

    for step in range(1, PLANE):
        slot = (place + step) % PLANE
        o_copy(slot, slot).wait_recv()
    for slot in range(PLANE):
        out_ref[:, slot * part:(slot + 1) * part] = obuf[slot]
    for step in range(1, shares):
        gated_copy(step, mine).wait_send()
    for step in range(1, PLANE):
        slot = (place + step) % PLANE
        k_copy(slot, place).wait_send()
        q_copy(slot, place).wait_send()
        o_copy(slot, place).wait_send()
    for slot in range(PLANE):
        pass_on(slot, lambda c: c.wait_send())


def attended(gated, values, proj_qk, count, shares):
    width = gated.shape[1]
    heads, part = width // HEAD, width // PLANE
    channels = proj_qk.shape[0]
    by_head = proj_qk.reshape(channels, 2, heads, HEAD).transpose(0, 2, 1, 3)
    vmem = pl.BlockSpec(memory_space=pltpu.VMEM)
    dma = pltpu.SemaphoreType.DMA
    return pl.pallas_call(
        functools.partial(attend_kernel, count, shares),
        out_shape=jax.ShapeDtypeStruct((FLEN, width), BF16),
        in_specs=[vmem, vmem, pl.BlockSpec(memory_space=pl.ANY)],
        out_specs=vmem,
        scratch_shapes=[
            pltpu.VMEM((shares, FLEN, width), BF16),
            pltpu.VMEM((2 * FLEN, 2 * width), BF16),
            pltpu.VMEM((heads, channels, 2, HEAD), BF16),
            pltpu.VMEM((heads // 2, 2 * FLEN, 2 * HEAD), F32),
            pltpu.VMEM((PLANE, FLEN, part), BF16),
            pltpu.VMEM((PLANE, FLEN, part), BF16),
            pltpu.VMEM((PLANE, FLEN, part), BF16),
            pltpu.VMEM((SLOTS * FLEN, part), BF16),
            pltpu.VMEM((PLANE, FLEN, part), BF16),
            pltpu.VMEM((PLANE, FLEN, part), BF16),
            dma((shares,)), dma((shares,)), dma((shares, heads)),
            dma((PLANE,)), dma((PLANE,)), dma((PLANE,)), dma((SLOTS,)),
            dma((2, PLANE)), dma((PLANE,)), dma((PLANE,)),
        ],
        compiler_params=pltpu.CompilerParams(
            collective_id=1, has_side_effects=True, vmem_limit_bytes=60 << 20
        ),
        name="project_and_attend",
    )(gated, values, by_head)


def shards(token_ids, stream_table, filters, proj_qk):
    count, shares = lax.axis_size("ctx"), lax.axis_size("tp")
    ids = share_ids(token_ids, count)
    gated, values = gated_and_values(ids, stream_table, filters)
    return attended(gated, values, proj_qk, count, shares)


def solution(mesh):
    placed = (P("ctx"), P(None, None, "tp"), P("tp", None), P(None, None, "tp"))
    return jax.shard_map(
        shards, mesh=mesh, in_specs=placed, out_specs=P("ctx", "tp"), check_vma=False
    )
```

time: 288 us -> 129 us (0.45)
  the two profiles are of different devices: /device:TPU:11 before, /device:TPU:31 now
where the time goes in v1:
time: 129 us
  Pallas kernels  121 us (94%)
  local copies, waits for them, and re-layouts  8.1 us (6%)
    pallas_call x1, Pallas kernels, attended(): pl.pallas_call(functools.partial(attend_kernel, count, shares), out_shape...  76.2 us
    pallas_call x1, Pallas kernels, gated_and_values(): pl.pallas_call(conv_kernel, out_shape=(jax.ShapeDtypeStruct((FLEN, width)...  37.6 us
    unnamed x11, local copies, waits for them, and re-layouts  8.1 us
    pallas_call x1, Pallas kernels, share_ids(): pl.pallas_call(functools.partial(ids_kernel, count), out_shape=jax.ShapeD...  6.84 us

profile of v1, /device:TPU:31, one launch (start us, length us, event | category | flops | bytes accessed | tf_op | source)
XLA Modules:
  0.0 128.8 jit_solution(2170998419807944384)
XLA Ops:
  0.0 6.8 %share_ids.1.ids_ref = s32[12,1,128]{2,1,0:T(1,128)} custom-call(s32[1,128]{1,0:T(1,128)} %bitcast.5), custom_call_target="tpu_custom_call" | custom-call | tf_op jit(solution)/shard_map/share_ids/pallas_call | solution.py:86
  6.9 0.0 copy-start
  6.9 2.8 %copy-done = bf16[3,512,2048]{2,1,0:T(8,128)(2,1)S(1)} copy-done((bf16[3,512,2048]{2,1,0:T(8,128)(2,1)S(1)}, bf16[3,512,2048]{2,1,0:T(8,128)(2,1)}, u32[]{:S(2)}) %copy-start) | copy-done | bytes 6291480
  9.6 0.0 copy-start.3
  9.6 0.8 copy-done.3
  10.5 0.0 copy-start.4
  10.5 0.7 copy-done.4
  11.2 37.6 %gated_and_values.1 = (bf16[128,2048]{1,0:T(8,128)(2,1)S(1)}, bf16[1408,512]{1,0:T(8,128)(2,1)S(1)}) custom-call(s32[12,1,128]{2,1,0:T(1,128)S(1)} %copy-done.4, bf16[3,512,2048]{2,1,0:T(8,128)(2,1)S(1)} %copy-done, f32[128,128]{1,0:T(8,128)S(1)} %copy-done.3), custom_call_target="tpu_custom_call" | custom-call | tf_op jit(solution)/shard_map/gated_and_values/pallas_call | solution.py:176
  48.8 0.0 copy-start.1
  48.8 1.1 copy-done.1
  49.9 0.0 copy-start.2
  49.9 0.8 copy-done.2
  50.7 76.2 %project_and_attend.1 = bf16[128,2048]{1,0:T(8,128)(2,1)} custom-call(bf16[128,2048]{1,0:T(8,128)(2,1)} %copy-done.2, bf16[1408,512]{1,0:T(8,128)(2,1)} %copy-done.1, bf16[4096,16,2,128]{3,2,1,0:T(2,128)(2,1)} %bitcast.4), custom_call_target="tpu_custom_call" | custom-call | tf_op jit(solution)/shard_map/project_and_attend/pallas_call | solution.py:386
  126.9 1.9 %copy.6 = bf16[128,2048]{1,0:T(8,128)(2,1)} copy(bf16[128,2048]{1,0:T(8,128)(2,1)} %project_and_attend.1) | data formatting | bytes 1048576
Async XLA Ops:
  6.9 2.8 %copy-start = (bf16[3,512,2048]{2,1,0:T(8,128)(2,1)S(1)}, bf16[3,512,2048]{2,1,0:T(8,128)(2,1)}, u32[]{:S(2)}) copy-start(bf16[3,512,2048]{2,1,0:T(8,128)(2,1)} %table_ref.1) | copy-start | bytes 18874372
  9.6 0.8 copy-start.3
  10.5 0.7 copy-start.4
  48.8 1.1 copy-start.1
  49.9 0.8 copy-start.2

commit v2 on v1

v2 whole, which is shorter than its diff:
```python
import functools
import jax
import jax.numpy as jnp
from jax import lax
from jax.experimental import pallas as pl
from jax.experimental.pallas import tpu as pltpu
from jax.sharding import PartitionSpec as P

HEAD = 128
GROUP = 16
FLEN = 128
SPAN = 8
LANE = 128
PLANE = 4
BACK = SPAN - 1
SLOTS = BACK + PLANE
MESH = pl.DeviceIdType.MESH
F32, BF16 = jnp.float32, jnp.bfloat16


def lanes(index, width=LANE):
    return pl.ds(pl.multiple_of(index * width, LANE), width)


def rows(index, count=1):
    return pl.ds(pl.multiple_of(index * FLEN, FLEN), count * FLEN)


def dot(a, b):
    return jnp.dot(a, b, preferred_element_type=F32)


def wait_ahead(barrier, ahead, always, each):
    for planes in range(3):
        @pl.when(ahead == planes if planes < 2 else ahead >= planes)
        def _():
            pl.semaphore_wait(barrier, always + planes * each)


def whole_kernel(
    count, shares, ids_ref, taps_ref, table_ref, weight_ref, out_ref,
    idbuf, table, onehot, toep, mixed, post, values,
    gall, wide, held, acc, qsend, ksend, qbuf, kbuf, osend, obuf,
    ts, isend, irecv, gs, gr, ws, qs, qr, ks, kr, zs, os_, or_,
):
    width = out_ref.shape[1]
    heads = width // HEAD
    part = width // PLANE
    heads_part = heads // PLANE
    vocab = table.shape[1]
    me, mine = lax.axis_index("ctx"), lax.axis_index("tp")
    plane, place = me // PLANE, me % PLANE
    planes = count // PLANE

    def table_copy(stream):
        return pltpu.make_async_copy(table_ref.at[stream], table.at[stream], ts.at[stream])

    def weights_copy(share, head):
        return pltpu.make_async_copy(
            weight_ref.at[pl.ds(share * width, width), head],
            held.at[head, pl.ds(share * width, width)],
            ws.at[share, head],
        )

    for stream in range(3):
        table_copy(stream).start()
    for step in range(shares):
        for head in range(heads):
            weights_copy((mine + step) % shares, head).start()

    idbuf[...] = jnp.full(idbuf.shape, -1, jnp.int32)
    idbuf[2 * PLANE + place] = ids_ref[...]
    kbuf[:BACK * FLEN] = jnp.zeros((BACK * FLEN, part), BF16)
    barrier = pltpu.get_barrier_semaphore()

    def greet(**device):
        pl.semaphore_signal(barrier, inc=1, device_id=device, device_id_type=MESH)

    def partners(sign, act):
        for dist in range(3):
            for other in range(PLANE):
                there = plane + sign * dist
                ok = (there >= 0) & (there < planes)
                if dist == 0:
                    ok = ok & (other != place)
                pl.when(ok)(functools.partial(act, dist, other, there * PLANE + other))

    for step in range(1, shares):
        greet(tp=(mine + step) % shares)
    partners(-1, lambda dist, other, device: greet(ctx=device))
    ahead = planes - 1 - plane
    for some in range(3):
        @pl.when(ahead == some if some < 2 else ahead >= some)
        def _():
            pl.semaphore_wait(barrier, shares - 1 + PLANE - 1 + some * PLANE)

    def remote(src, dst, send, recv, **device):
        return pltpu.make_async_remote_copy(
            src_ref=src, dst_ref=dst, send_sem=send, recv_sem=recv, device_id=device, device_id_type=MESH
        )

    def ids_copy(dist, other, device):
        slot = 2 * PLANE + place - dist * PLANE
        return remote(ids_ref, idbuf.at[slot], isend.at[dist * PLANE + other], irecv.at[slot], ctx=device)

    def ids_here(dist, other, device):
        slot = 2 * PLANE + other - dist * PLANE
        remote(ids_ref, idbuf.at[slot], isend.at[0], irecv.at[slot], ctx=device).wait_recv()

    partners(1, lambda *a: ids_copy(*a).start())
    partners(-1, ids_here)

    def mark(block, _):
        ids = jnp.transpose(jnp.broadcast_to(idbuf[block].astype(F32), (FLEN, FLEN)))
        word = lax.broadcasted_iota(jnp.int32, (FLEN, LANE), 1).astype(F32)
        for at in range(vocab // LANE):
            onehot[rows(block), at * LANE:(at + 1) * LANE] = (ids == word + float(at * LANE)).astype(F32).astype(BF16)
        return 0

    lax.fori_loop(BACK + place, BACK + place + 2, mark, 0)
    row = lax.broadcasted_iota(jnp.int32, (FLEN, FLEN), 0)
    col = lax.broadcasted_iota(jnp.int32, (FLEN, FLEN), 1)
    flip = ((row + col == FLEN) | (row + col == 0)).astype(F32).astype(BF16)
    after = (row >= col).astype(F32).astype(BF16)
    before = (row < col).astype(F32).astype(BF16)
    per = LANE // GROUP

    def build(column):
        line = dot(taps_ref[pl.ds(pl.multiple_of(column * per, per), per), :].astype(BF16), flip)
        for g in range(per):
            turned = pltpu.roll(
                jnp.broadcast_to(line[g:g + 1], (FLEN, FLEN)), 0, 1, stride=1, stride_axis=0
            ).astype(BF16)
            toep[g * FLEN:(g + 1) * FLEN, :FLEN] = turned * before
            toep[g * FLEN:(g + 1) * FLEN, FLEN:] = turned * after

    def convolve(window):
        group_of = lax.broadcasted_iota(jnp.int32, (FLEN, window.shape[1]), 1) % LANE // GROUP
        total = dot(toep[:FLEN], window)
        for g in range(1, per):
            total = jnp.where(group_of == g, dot(toep[g * FLEN:(g + 1) * FLEN], window), total)
        return total

    def pair_of(cols):
        return jnp.concatenate([table[1, :, cols], table[2, :, cols]], axis=1)

    def own(column, _):
        cols = lanes(column)
        both = dot(onehot[rows(BACK + place, 2), :], pair_of(cols))
        window = (both[:, :LANE] * both[:, LANE:]).astype(BF16)
        gate = dot(onehot[rows(BACK + 1 + place), :], table[0, :, cols])
        build(column)
        gall[mine, :, cols] = (gate * convolve(window)).astype(BF16)
        return 0

    def gated_copy(step, slot, piece):
        cut = gall.at[slot, :, piece * part:(piece + 1) * part]
        return remote(cut, cut, gs.at[step, piece], gr.at[slot, piece], tp=(mine + step) % shares)

    for stream in range(3):
        table_copy(stream).wait()
    for piece in range(PLANE):
        lax.fori_loop(piece * (part // LANE), (piece + 1) * (part // LANE), own, 0)
        for step in range(1, shares):
            gated_copy(step, mine, piece).start()

    def shared(step):
        column = place * (part // LANE) + step
        cols = lanes(column)
        build(column)

        def fill(some, _):
            marks = onehot[pl.ds(pl.multiple_of(some * PLANE * FLEN, FLEN), PLANE * FLEN), :]
            here = pl.ds(pl.multiple_of(some * PLANE * FLEN, FLEN), PLANE * FLEN)
            both = dot(marks, pair_of(cols))
            mixed[here, :] = (both[:, :LANE] * both[:, LANE:]).astype(BF16)
            post[here, :] = dot(marks, table[0, :, cols])
            return 0

        lax.fori_loop(0, 3, fill, 0)

        def two_windows(twice, _):
            block = 2 * twice
            conv = convolve(jnp.concatenate([mixed[rows(block, 2), :], mixed[rows(block + 1, 2), :]], axis=1))
            values[rows(block), step * LANE:(step + 1) * LANE] = (post[rows(block + 1), :] * conv[:, :LANE]).astype(BF16)
            values[rows(block + 1), step * LANE:(step + 1) * LANE] = (post[rows(block + 2), :] * conv[:, LANE:]).astype(BF16)
            return 0

        lax.fori_loop(0, SLOTS // 2, two_windows, 0)
        conv = convolve(mixed[(SLOTS - 1) * FLEN:(SLOTS + 1) * FLEN, :])
        values[(SLOTS - 1) * FLEN:, step * LANE:(step + 1) * LANE] = (post[SLOTS * FLEN:, :] * conv).astype(BF16)

    src = lax.broadcasted_iota(jnp.int32, (LANE, 4 * LANE), 0)
    dst = lax.broadcasted_iota(jnp.int32, (LANE, 4 * LANE), 1)
    spread = (dst == jnp.where(dst < 2 * LANE, 2 * src, 2 * src + 1 + 2 * LANE)).astype(F32).astype(BF16)
    paired = held.reshape(heads, 2 * shares * width, HEAD)
    depth = min(2 * width, 1024)

    def q_copy(group, slot):
        return remote(qsend.at[group], qbuf.at[slot], qs.at[group], qr.at[slot], ctx=plane * PLANE + group)

    def k_copy(group, slot):
        return remote(ksend.at[group], kbuf.at[rows(BACK + slot)], ks.at[group], kr.at[BACK + slot], ctx=plane * PLANE + group)

    def z_copy(dist, slot):
        to = BACK + slot - dist * PLANE
        return remote(kbuf.at[rows(BACK + slot)], kbuf.at[rows(to)], zs.at[dist - 1, slot], kr.at[to], ctx=me + dist * PLANE)

    def pass_on(slot, act):
        @pl.when(plane + 1 < planes)
        def _():
            act(z_copy(1, slot))

        @pl.when((plane + 2 < planes) & (slot >= 1))
        def _():
            act(z_copy(2, slot))

    def project(step, share, head):
        base = share * 2 * width

        def chunk(at, total):
            take = pl.ds(pl.multiple_of(base + at * depth, LANE), depth)
            block = jnp.concatenate([paired[head, take, :], paired[head + 1, take, :]], axis=1)
            return total + dot(wide[:, lanes(at, depth)], block)

        first = jnp.zeros((2 * FLEN, 2 * HEAD), F32) if step == 0 else acc[head // 2]
        return lax.fori_loop(0, 2 * width // depth, chunk, first)

    for step in range(shares):
        share = (mine + step) % shares
        if step > 0:
            for piece in range(PLANE):
                gated_copy(step, share, piece).wait_recv()

        def widen(column, _):
            both = dot(gall[share, :, lanes(column)], spread).astype(BF16)
            wide[:FLEN, lanes(column, 2 * LANE)] = both[:, :2 * LANE]
            wide[FLEN:, lanes(column, 2 * LANE)] = both[:, 2 * LANE:]
            return 0

        lax.fori_loop(0, width // LANE, widen, 0)
        for head in range(0, heads, 2):
            weights_copy(share, head).wait()
            weights_copy(share, head + 1).wait()
            total = project(step, share, head)
            if step < shares - 1:
                acc[head // 2] = total
                continue
            for one in range(2):
                group, at = (head + one) // heads_part, (head + one) % heads_part
                cut = total[:, one * HEAD:(one + 1) * HEAD].astype(BF16)
                qsend[group, :, at * HEAD:(at + 1) * HEAD] = cut[:FLEN]
                ksend[group, :, at * HEAD:(at + 1) * HEAD] = cut[FLEN:]
                if at == heads_part - 1:
                    @pl.when(group != place)
                    def _():
                        k_copy(group, place).start()
                        q_copy(group, place).start()

                    @pl.when(group == place)
                    def _():
                        kbuf[rows(BACK + place), :] = ksend[group]
                        qbuf[place] = qsend[group]
                        pass_on(place, lambda c: c.start())

    lax.fori_loop(0, 3 * PLANE, mark, 0)
    for column in range(part // LANE):
        shared(column)
        if column == 0:
            for step in range(1, PLANE):
                slot = (place + step) % PLANE
                k_copy(slot, slot).wait_recv()
                pass_on(slot, lambda c: c.start())
    for step in range(1, PLANE):
        slot = (place + step) % PLANE
        q_copy(slot, slot).wait_recv()
    for dist in (1, 2):
        @pl.when(plane >= dist)
        def _():
            for slot in range(dist - 1, PLANE):
                z_copy(dist, slot).wait_recv()

    def o_copy(group, slot):
        return remote(osend.at[group], obuf.at[slot], os_.at[group], or_.at[slot], ctx=plane * PLANE + group)

    key_at = lax.broadcasted_iota(jnp.int32, (FLEN, SPAN * FLEN), 1)
    query_at = lax.broadcasted_iota(jnp.int32, (FLEN, SPAN * FLEN), 0)
    for block in range(PLANE):
        least = (BACK - block - plane * PLANE) * FLEN
        allowed = (key_at <= query_at + BACK * FLEN) & (key_at >= least)

        def one_head(head, _):
            keys = kbuf[block * FLEN:(block + SPAN) * FLEN, lanes(head)]
            seen = values[block * FLEN:(block + SPAN) * FLEN, lanes(head)]
            scores = lax.dot_general(
                qbuf[block, :, lanes(head)], keys, (((1,), (1,)), ((), ())), preferred_element_type=F32
            ) * HEAD ** (-0.5)
            scores = jnp.where(allowed, scores, -1e30)
            weights = jnp.exp(scores - jnp.max(scores, axis=1, keepdims=True))
            row_sum = jnp.sum(weights, axis=1, keepdims=True)
            osend[block, :, lanes(head)] = (dot(weights.astype(BF16), seen) / row_sum).astype(BF16)
            return 0

        lax.fori_loop(0, heads_part, one_head, 0)

        @pl.when(block != place)
        def _():
            o_copy(block, place).start()

        @pl.when(block == place)
        def _():
            obuf[place] = osend[block]

    for step in range(1, PLANE):
        slot = (place + step) % PLANE
        o_copy(slot, slot).wait_recv()
    for slot in range(PLANE):
        out_ref[:, slot * part:(slot + 1) * part] = obuf[slot]
    for step in range(1, shares):
        for piece in range(PLANE):
            gated_copy(step, mine, piece).wait_send()
    partners(1, lambda *a: ids_copy(*a).wait_send())
    for step in range(1, PLANE):
        slot = (place + step) % PLANE
        k_copy(slot, place).wait_send()
        q_copy(slot, place).wait_send()
        o_copy(slot, place).wait_send()
    for slot in range(PLANE):
        pass_on(slot, lambda c: c.wait_send())


def shards(token_ids, stream_table, filters, proj_qk):
    count, shares = lax.axis_size("ctx"), lax.axis_size("tp")
    width, vocab = stream_table.shape[2], stream_table.shape[1]
    heads, part = width // HEAD, width // PLANE
    channels = proj_qk.shape[0]
    by_head = proj_qk.reshape(channels, 2, heads, HEAD).transpose(0, 2, 1, 3)
    vmem, hbm = pl.BlockSpec(memory_space=pltpu.VMEM), pl.BlockSpec(memory_space=pl.ANY)
    dma = pltpu.SemaphoreType.DMA
    return pl.pallas_call(
        functools.partial(whole_kernel, count, shares),
        out_shape=jax.ShapeDtypeStruct((FLEN, width), BF16),
        in_specs=[vmem, vmem, hbm, hbm],
        out_specs=vmem,
        scratch_shapes=[
            pltpu.VMEM((3 * PLANE, 1, FLEN), jnp.int32),
            pltpu.VMEM((3, vocab, width), BF16),
            pltpu.VMEM((3 * PLANE * FLEN, vocab), BF16),
            pltpu.VMEM((LANE // GROUP * FLEN, 2 * FLEN), BF16),
            pltpu.VMEM((3 * PLANE * FLEN, LANE), BF16),
            pltpu.VMEM((3 * PLANE * FLEN, LANE), F32),
            pltpu.VMEM((SLOTS * FLEN, part), BF16),
            pltpu.VMEM((shares, FLEN, width), BF16),
            pltpu.VMEM((2 * FLEN, 2 * width), BF16),
            pltpu.VMEM((heads, channels, 2, HEAD), BF16),
            pltpu.VMEM((heads // 2, 2 * FLEN, 2 * HEAD), F32),
            pltpu.VMEM((PLANE, FLEN, part), BF16),
            pltpu.VMEM((PLANE, FLEN, part), BF16),
            pltpu.VMEM((PLANE, FLEN, part), BF16),
            pltpu.VMEM((SLOTS * FLEN, part), BF16),
            pltpu.VMEM((PLANE, FLEN, part), BF16),
            pltpu.VMEM((PLANE, FLEN, part), BF16),
            dma((3,)), dma((3 * PLANE,)), dma((3 * PLANE,)),
            dma((shares, PLANE)), dma((shares, PLANE)), dma((shares, heads)),
            dma((PLANE,)), dma((PLANE,)), dma((PLANE,)), dma((SLOTS,)),
            dma((2, PLANE)), dma((PLANE,)), dma((PLANE,)),
        ],
        compiler_params=pltpu.CompilerParams(
            collective_id=0, has_side_effects=True, vmem_limit_bytes=60 << 20
        ),
        name="hyena_attention",
    )(token_ids.reshape(1, FLEN), filters, stream_table, by_head)


def solution(mesh):
    placed = (P("ctx"), P(None, None, "tp"), P("tp", None), P(None, None, "tp"))
    return jax.shard_map(
        shards, mesh=mesh, in_specs=placed, out_specs=P("ctx", "tp"), check_vma=False
    )
```

time: 129 us -> 103 us (0.80)
  Pallas kernels: 121 us -> 101 us
  local copies, waits for them, and re-layouts: 8.1 us -> 1.88 us
    pallas_call x3 -> x1, Pallas kernels: 121 us -> 101 us  [shards(): pl.pallas_call(functools.partial(whole_kernel, count, shares), out_shape=...]
    unnamed x11 -> x1, local copies, waits for them, and re-layouts: 8.1 us -> 1.88 us
where the time goes in v2:
time: 103 us
  Pallas kernels  101 us (98%)
  local copies, waits for them, and re-layouts  1.88 us (2%)
    pallas_call x1, Pallas kernels, shards(): pl.pallas_call(functools.partial(whole_kernel, count, shares), out_shape=...  101 us

profile of v2, /device:TPU:31, one launch (start us, length us, event | category | flops | bytes accessed | tf_op | source)
XLA Modules:
  0.0 102.7 jit_solution(8272738335130125241)
XLA Ops:
  0.0 100.8 %hyena_attention.1 = bf16[128,2048]{1,0:T(8,128)(2,1)} custom-call(s32[1,128]{1,0:T(1,128)} %bitcast.5, f32[128,128]{1,0:T(8,128)} %taps_ref.1, bf16[3,512,2048]{2,1,0:T(8,128)(2,1)} %table_ref.1, bf16[4096,16,2,128]{3,2,1,0:T(2,128)(2,1)} %bitcast.4), custom_call_target="tpu_custom_call" | custom-call | tf_op jit(solution)/shard_map/hyena_attention/pallas_call | solution.py:340
  100.8 1.9 %copy.6 = bf16[128,2048]{1,0:T(8,128)(2,1)} copy(bf16[128,2048]{1,0:T(8,128)(2,1)} %hyena_attention.1) | data formatting | bytes 1048576

commit v3 on v2

--- a/solution.py
+++ b/solution.py
@@ -55,18 +55,15 @@
     def table_copy(stream):
         return pltpu.make_async_copy(table_ref.at[stream], table.at[stream], ts.at[stream])
 
-    def weights_copy(share, head):
-        return pltpu.make_async_copy(
-            weight_ref.at[pl.ds(share * width, width), head],
-            held.at[head, pl.ds(share * width, width)],
-            ws.at[share, head],
-        )
+    def weights_copy(share, piece):
+        cut = pl.ds(share * width + piece * part, part)
+        return pltpu.make_async_copy(weight_ref.at[cut], held.at[cut], ws.at[share, piece])
 
     for stream in range(3):
         table_copy(stream).start()
     for step in range(shares):
-        for head in range(heads):
-            weights_copy((mine + step) % shares, head).start()
+        for piece in range(PLANE):
+            weights_copy((mine + step) % shares, piece).start()
 
     idbuf[...] = jnp.full(idbuf.shape, -1, jnp.int32)
     idbuf[2 * PLANE + place] = ids_ref[...]
@@ -136,9 +133,10 @@
 
     def convolve(window):
         group_of = lax.broadcasted_iota(jnp.int32, (FLEN, window.shape[1]), 1) % LANE // GROUP
-        total = dot(toep[:FLEN], window)
+        every = dot(toep[...], window)
+        total = every[:FLEN]
         for g in range(1, per):
-            total = jnp.where(group_of == g, dot(toep[g * FLEN:(g + 1) * FLEN], window), total)
+            total = jnp.where(group_of == g, every[g * FLEN:(g + 1) * FLEN], total)
         return total
 
     def pair_of(cols):
@@ -193,7 +191,6 @@
     src = lax.broadcasted_iota(jnp.int32, (LANE, 4 * LANE), 0)
     dst = lax.broadcasted_iota(jnp.int32, (LANE, 4 * LANE), 1)
     spread = (dst == jnp.where(dst < 2 * LANE, 2 * src, 2 * src + 1 + 2 * LANE)).astype(F32).astype(BF16)
-    paired = held.reshape(heads, 2 * shares * width, HEAD)
     depth = min(2 * width, 1024)
 
     def q_copy(group, slot):
@@ -216,11 +213,11 @@
             act(z_copy(2, slot))
 
     def project(step, share, head):
-        base = share * 2 * width
-
         def chunk(at, total):
-            take = pl.ds(pl.multiple_of(base + at * depth, LANE), depth)
-            block = jnp.concatenate([paired[head, take, :], paired[head + 1, take, :]], axis=1)
+            take = pl.ds(share * width + at * (depth // 2), depth // 2)
+            block = jnp.concatenate(
+                [held[take, head].reshape(depth, HEAD), held[take, head + 1].reshape(depth, HEAD)], axis=1
+            )
             return total + dot(wide[:, lanes(at, depth)], block)
 
         first = jnp.zeros((2 * FLEN, 2 * HEAD), F32) if step == 0 else acc[head // 2]
@@ -239,9 +236,9 @@
             return 0
 
         lax.fori_loop(0, width // LANE, widen, 0)
+        for piece in range(PLANE):
+            weights_copy(share, piece).wait()
         for head in range(0, heads, 2):
-            weights_copy(share, head).wait()
-            weights_copy(share, head + 1).wait()
             total = project(step, share, head)
             if step < shares - 1:
                 acc[head // 2] = total
@@ -352,7 +349,7 @@
             pltpu.VMEM((SLOTS * FLEN, part), BF16),
             pltpu.VMEM((shares, FLEN, width), BF16),
             pltpu.VMEM((2 * FLEN, 2 * width), BF16),
-            pltpu.VMEM((heads, channels, 2, HEAD), BF16),
+            pltpu.VMEM((channels, heads, 2, HEAD), BF16),
             pltpu.VMEM((heads // 2, 2 * FLEN, 2 * HEAD), F32),
             pltpu.VMEM((PLANE, FLEN, part), BF16),
             pltpu.VMEM((PLANE, FLEN, part), BF16),
@@ -361,7 +358,7 @@
             pltpu.VMEM((PLANE, FLEN, part), BF16),
             pltpu.VMEM((PLANE, FLEN, part), BF16),
             dma((3,)), dma((3 * PLANE,)), dma((3 * PLANE,)),
-            dma((shares, PLANE)), dma((shares, PLANE)), dma((shares, heads)),
+            dma((shares, PLANE)), dma((shares, PLANE)), dma((shares, PLANE)),
             dma((PLANE,)), dma((PLANE,)), dma((PLANE,)), dma((SLOTS,)),
             dma((2, PLANE)), dma((PLANE,)), dma((PLANE,)),
         ],

time: 103 us -> 98.6 us (0.957)
  Pallas kernels: 101 us -> 96.5 us
    pallas_call x1, Pallas kernels: 101 us -> 96.5 us  [shards(): pl.pallas_call(functools.partial(whole_kernel, count, shares), out_shape=...]
where the time goes in v3:
time: 98.6 us; the launch traced here: 98.4 us
  Pallas kernels  96.5 us (98%)
  local copies, waits for them, and re-layouts  1.88 us (2%)
    pallas_call x1, Pallas kernels, shards(): pl.pallas_call(functools.partial(whole_kernel, count, shares), out_shape=...  96.5 us

profile of v3, /device:TPU:31, one launch (start us, length us, event | category | flops | bytes accessed | tf_op | source)
XLA Modules:
  0.0 98.4 jit_solution(7365618701295321749)
XLA Ops:
  0.0 96.5 %hyena_attention.1 = bf16[128,2048]{1,0:T(8,128)(2,1)} custom-call(s32[1,128]{1,0:T(1,128)} %bitcast.5, f32[128,128]{1,0:T(8,128)} %taps_ref.1, bf16[3,512,2048]{2,1,0:T(8,128)(2,1)} %table_ref.1, bf16[4096,16,2,128]{3,2,1,0:T(2,128)(2,1)} %bitcast.4), custom_call_target="tpu_custom_call" | custom-call | tf_op jit(solution)/shard_map/hyena_attention/pallas_call | solution.py:337
  96.5 1.9 %copy.6 = bf16[128,2048]{1,0:T(8,128)(2,1)} copy(bf16[128,2048]{1,0:T(8,128)(2,1)} %hyena_attention.1) | data formatting | bytes 1048576
